TPU v7x, 32 devices: a whole 2x2x4 slice. The times are simulated.
32 devices in a mesh: dp: 8 (over z, y), row: 2 (over core), col: 2 (over x).
Axes of the slice: x: 2, y: 2, z: 4, core: 2. Of those that a mesh axis runs over, the one named last changes fastest.
Arguments:
- block_input: bfloat16 [4096, 2560], P(('dp', 'col')), may hold values from -6 to 6
- cotangent: bfloat16 [4096, 2560], P(('dp', 'col'), 'row'), may hold values from -6 to 6
- seq_lengths: int32 [32], replicated, may hold values from 16 to 128, as said below
- seq_owner: int32 [32], replicated, may hold values from 0 to 15, as said below
- norm_gain: bfloat16 [2560], P('row'), may hold values from 0.5 to 1.5
- proj_zx: bfloat16 [2560, 2, 5120], P('row', None, 'col'), may hold values from -0.125 to 0.125
- proj_bc: bfloat16 [2560, 256], P('row'), may hold values from -0.125 to 0.125
- proj_dt: bfloat16 [2560, 80], P('row', 'col'), may hold values from -0.125 to 0.125
- proj_out: bfloat16 [5120, 2560], P('col', 'row'), may hold values from -0.078125 to 0.078125
- inner_kernel: float32 [4, 5120], P(None, 'col'), may hold values from -3 to 3
- inner_offset: float32 [5120], P('col'), may hold values from -1.5 to 1.5
- shared_kernel: float32 [4, 256], replicated, may hold values from -3 to 3
- shared_offset: float32 [256], replicated, may hold values from -1.5 to 1.5
- decay_log: float32 [80], P('col'), may hold values from 0 to 2.77
- step_bias: float32 [80], P('col'), may hold values from -6 to -2
- skip_gain: float32 [80], P('col'), may hold values from 0.5 to 1.5
- output_gain: bfloat16 [5120], P('col'), may hold values from 0.5 to 1.5
Outputs:
- block_output: bfloat16 [4096, 2560], P(('dp', 'col'), 'row')
- input_grad: float32 [4096, 2560], P(('dp', 'col'), 'row')
- grad_norm: float32 [2560], P('row')
- grad_inproj: float32 [2560, 2, 5120], P('row', None, 'col')
- grad_shared: float32 [2560, 256], P('row')
- grad_steps: float32 [2560, 80], P('row', 'col')
- grad_outproj: float32 [5120, 2560], P('col', 'row')
- grad_kernel: float32 [4, 5120], P(None, 'col')
- grad_offset: float32 [5120], P('col')
- grad_skernel: float32 [4, 256], replicated
- grad_soffset: float32 [256], replicated
- grad_decay: float32 [80], P('col')
- grad_stepbias: float32 [80], P('col')
- grad_skip: float32 [80], P('col')
- grad_ogain: float32 [5120], P('col')
Inputs may be any that keep to these rules, and one draw needn't show every extreme that they name: `seq_lengths`: the lengths of the 2 sequences of one bucket sum to at most 256; in every draw some bucket holds 2 sequences of exactly 128 rows, so that its sum is 256. `seq_owner`: every bucket owns exactly 2 sequences.
All inputs are finite; a program needn't handle non-finite values.
Results may differ from a plain program's by a relative error of at most 0.0079.
The roundings to bfloat16 on the way count: a program that leaves them out, or rounds other values in their place, can miss the bound.
Values may be sent and summed in bfloat16 or wider, within the bound.
A program may use at most 256 MiB of HBM per device.

v0:
```python
import jax
import jax.numpy as jnp
from jax import lax
from jax.sharding import PartitionSpec as P

D = 2560
DI = 5120
CAP = 256
EPSILON = 1e-05
PRECISE = lax.Precision.HIGHEST


def layout(seq_lengths, seq_owner, bucket, capacity):
    owned = seq_owner == bucket
    owned_len = jnp.where(owned, seq_lengths, 0)
    order = jnp.arange(seq_lengths.shape[0], dtype=jnp.int32)
    starts = jnp.sum(jnp.where(order[None, :] < order[:, None], owned_len[None, :], 0), axis=1)
    places = jnp.arange(capacity, dtype=jnp.int32)[:, None]
    ends = starts + seq_lengths
    inside = owned[None, :] & (places >= starts[None, :]) & (places < ends[None, :])
    live_rows = jnp.any(inside, axis=1)
    seq_index = jnp.arange(seq_lengths.shape[0], dtype=jnp.int32)
    seq_ids = jnp.sum(jnp.where(inside, seq_index[None, :], 0), axis=1)
    seq_ids = jnp.where(live_rows, seq_ids, -1)
    return (seq_ids, live_rows.astype(jnp.float32))


def convolve(channels, kernel, offset, seq_ids, live_rows):
    tap_count = kernel.shape[0]
    summed_in = offset[None, :] + kernel[tap_count - 1][None, :] * channels
    for lag_steps in range(1, tap_count):
        lagged = jnp.concatenate(
            [jnp.zeros((lag_steps, channels.shape[1]), jnp.float32), channels[:-lag_steps]], axis=0
        )
        prior_ids = jnp.concatenate([jnp.full((lag_steps,), -1, jnp.int32), seq_ids[:-lag_steps]])
        same_seq = jnp.where((prior_ids == seq_ids) & (live_rows > 0), 1.0, 0.0).astype(jnp.float32)
        summed_in = (
            summed_in + kernel[tap_count - 1 - lag_steps][None, :] * lagged * same_seq[:, None]
        )
    return summed_in


def mix_bucket(values, bmat, cmat, sizes, rates, skip_gain, ids, live):
    rows_all, head_count, head_dim = values.shape
    lower = jnp.arange(rows_all)[:, None] >= jnp.arange(rows_all)[None, :]
    cumulated = jnp.dot(lower.astype(jnp.float32), rates, precision=PRECISE)
    pair_live = (ids[:, None] == ids[None, :]) & (live[:, None] > 0) & (live[None, :] > 0) & lower
    scores = jnp.dot(cmat, bmat.T, precision=PRECISE)
    gap = jnp.where(pair_live[:, :, None], cumulated[:, None, :] - cumulated[None, :, :], 0.0)
    weights = (
        jnp.exp(gap) * (pair_live.astype(jnp.float32) * scores)[:, :, None] * sizes[None, :, :]
    )
    within = jnp.einsum("tsh,shp->thp", weights, values, precision=PRECISE)
    mixed_out = (within + skip_gain[None, :, None] * values) * live[:, None, None]
    return mixed_out.reshape(rows_all, head_count * head_dim)


def sum_rows_over_dp(part, shared_cols=0):
    piece = lax.psum_scatter(part.astype(jnp.bfloat16), "dp", scatter_dimension=0, tiled=True)
    if shared_cols:
        own = piece.shape[1] - shared_cols
        tail = lax.psum(piece[:, own:].astype(jnp.float32), "col").astype(jnp.bfloat16)
        piece = jnp.concatenate([piece[:, :own], tail], axis=1)
    return lax.all_gather(piece, "dp", axis=0, tiled=True)


def mixer_local(
    conv_in,
    narrow_in,
    inner_kernel,
    inner_offset,
    shared_kernel,
    shared_offset,
    decay_log,
    step_bias,
    skip_gain,
    seq_ids,
    live_rows,
):
    inner_size = inner_kernel.shape[1]
    state_size = shared_kernel.shape[1] // 2
    head_count = decay_log.shape[0]
    shared_in = narrow_in[:, : 2 * state_size]
    step_raw = narrow_in[:, 2 * state_size :]
    mixed_x = jax.nn.silu(convolve(conv_in, inner_kernel, inner_offset, seq_ids, live_rows))
    mixed_bc = jax.nn.silu(convolve(shared_in, shared_kernel, shared_offset, seq_ids, live_rows))
    step_sizes = jax.nn.softplus(step_raw + step_bias[None, :])
    decay_rate = step_sizes * (-jnp.exp(decay_log))[None, :]
    values = mixed_x.reshape(mixed_x.shape[0], head_count, inner_size // head_count)
    return mix_bucket(
        values,
        mixed_bc[:, :state_size],
        mixed_bc[:, state_size:],
        step_sizes,
        decay_rate,
        skip_gain,
        seq_ids,
        live_rows,
    )


def per_device(
    block_input,
    cotangent,
    seq_lengths,
    seq_owner,
    norm_gain,
    proj_zx,
    proj_bc,
    proj_dt,
    proj_out,
    inner_kernel,
    inner_offset,
    shared_kernel,
    shared_offset,
    decay_log,
    step_bias,
    skip_gain,
    output_gain,
):
    row_count = lax.axis_size("row")
    col_count = lax.axis_size("col")
    row_index = lax.axis_index("row")
    col_index = lax.axis_index("col")
    data_index = lax.axis_index("dp")
    width_part = norm_gain.shape[0]
    inner_size = proj_zx.shape[2]
    state_size = proj_bc.shape[1] // 2
    tap_count = inner_kernel.shape[0]
    capacity = CAP
    bucket = data_index * row_count + row_index
    seq_ids, live_rows = layout(seq_lengths, seq_owner, bucket, capacity)
    rscale = lax.rsqrt(
        jnp.mean(jnp.square(block_input.astype(jnp.float32)), axis=1, keepdims=True) + EPSILON
    )
    own_cols = lax.dynamic_slice_in_dim(block_input, row_index * width_part, width_part, 1).astype(
        jnp.float32
    )
    normalized = own_cols * rscale
    gain_f = norm_gain.astype(jnp.float32)
    normed = (normalized * gain_f[None, :]).astype(jnp.bfloat16)
    normed_all = lax.all_gather(normed, "col", axis=0, tiled=True)
    weight_zx = proj_zx.reshape(width_part, 2 * inner_size)
    weight_narrow = jnp.concatenate([proj_bc, proj_dt], axis=1)
    zx_in = lax.psum_scatter(
        jnp.dot(normed_all, weight_zx, preferred_element_type=jnp.float32),
        "row",
        scatter_dimension=0,
        tiled=True,
    )
    narrow_in = lax.psum_scatter(
        jnp.dot(normed_all, weight_narrow, preferred_element_type=jnp.float32),
        "row",
        scatter_dimension=0,
        tiled=True,
    )
    gate_in = zx_in[:, :inner_size]
    conv_in = zx_in[:, inner_size:]

    def local_piece(*operands):
        return mixer_local(*operands, seq_ids, live_rows)

    ssm_rows, pull_back = jax.vjp(
        local_piece,
        conv_in,
        narrow_in,
        inner_kernel,
        inner_offset,
        shared_kernel,
        shared_offset,
        decay_log,
        step_bias,
        skip_gain,
    )
    gated_rows, gate_back = jax.vjp(
        lambda ssm_value, gate_value: ssm_value * jax.nn.silu(gate_value), ssm_rows, gate_in
    )
    square_sum = lax.psum(jnp.sum(gated_rows * gated_rows, axis=1), "col")
    rnorm = lax.rsqrt(square_sum / DI + EPSILON)[:, None]
    out_gain = output_gain.astype(jnp.float32)
    branch = (gated_rows * rnorm * out_gain[None, :]).astype(jnp.bfloat16)
    branch_all = lax.all_gather(branch, "row", axis=0, tiled=True)
    row_piece = branch_all
    branch_out = lax.psum_scatter(
        jnp.dot(row_piece, proj_out, preferred_element_type=jnp.float32),
        "col",
        scatter_dimension=0,
        tiled=True,
    )
    block_output = (own_cols + branch_out).astype(jnp.bfloat16)
    cot_all = lax.all_gather(cotangent, "col", axis=0, tiled=True)
    row_piece = cot_all
    branch_grad = lax.psum_scatter(
        lax.dot_general(
            row_piece, proj_out, (((1,), (1,)), ((), ())), preferred_element_type=jnp.float32
        ),
        "row",
        scatter_dimension=0,
        tiled=True,
    )
    outproj_part = lax.dot_general(
        branch_all, cot_all, (((0,), (0,)), ((), ())), preferred_element_type=jnp.float32
    )
    outproj_total = sum_rows_over_dp(outproj_part).astype(jnp.float32)
    scaled_grad = branch_grad * out_gain[None, :]
    cross_sum = lax.psum(jnp.sum(scaled_grad * gated_rows, axis=1), "col")
    gated_grad = rnorm * scaled_grad - gated_rows * rnorm**3 * (cross_sum / DI)[:, None]
    ogain_part = jnp.sum(branch_grad * gated_rows * rnorm, axis=0)
    ssm_grad, gate_grad = gate_back(gated_grad)
    gate_all = lax.all_gather(gate_grad.astype(jnp.bfloat16), "row", axis=0, tiled=True)
    gate_total = sum_rows_over_dp(
        lax.dot_general(
            normed_all, gate_all, (((0,), (0,)), ((), ())), preferred_element_type=jnp.float32
        )
    )
    local_grads = pull_back(ssm_grad)
    inner_all = lax.all_gather(local_grads[0].astype(jnp.bfloat16), "row", axis=0, tiled=True)
    narrow_all = lax.all_gather(local_grads[1].astype(jnp.bfloat16), "row", axis=0, tiled=True)
    normed_grad = lax.psum_scatter(
        lax.dot_general(
            jnp.concatenate([gate_all, inner_all], axis=1),
            weight_zx,
            (((1,), (1,)), ((), ())),
            preferred_element_type=jnp.float32,
        )
        + lax.dot_general(
            narrow_all, weight_narrow, (((1,), (1,)), ((), ())), preferred_element_type=jnp.float32
        ),
        "col",
        scatter_dimension=0,
        tiled=True,
    )
    inner_total = sum_rows_over_dp(
        lax.dot_general(
            normed_all, inner_all, (((0,), (0,)), ((), ())), preferred_element_type=jnp.float32
        )
    )
    narrow_part = lax.dot_general(
        normed_all, narrow_all, (((0,), (0,)), ((), ())), preferred_element_type=jnp.float32
    )
    narrow_total = sum_rows_over_dp(
        jnp.concatenate([narrow_part[:, 2 * state_size :], narrow_part[:, : 2 * state_size]], 1),
        2 * state_size,
    ).astype(jnp.float32)
    head_count = decay_log.shape[0]
    steps_total = narrow_total[:, :head_count]
    shared_total = narrow_total[:, head_count:]
    inproj_total = jnp.stack([gate_total, inner_total], axis=1).astype(jnp.float32)
    scaled_in = normed_grad * gain_f[None, :]
    norm_part = jnp.sum(normed_grad * normalized, axis=0)
    row_stat = lax.psum(jnp.sum(scaled_in * normalized, axis=1), "row")
    input_grad = cotangent.astype(jnp.float32) + rscale * (
        scaled_in - normalized * (row_stat / D)[:, None]
    )
    row_hot = (jnp.arange(row_count) == row_index).astype(jnp.float32)
    col_hot = (jnp.arange(col_count) == col_index).astype(jnp.float32)
    gain_slot = row_hot[:, None] * norm_part[None, :]
    head_stack = jnp.stack([local_grads[6], local_grads[7], local_grads[8]], axis=0)
    head_slot = col_hot[None, :, None] * head_stack[:, None, :]
    chan_stack = jnp.concatenate(
        [local_grads[2], local_grads[3][None, :], ogain_part[None, :]], axis=0
    )
    chan_slot = col_hot[None, :, None] * chan_stack[:, None, :]
    shared_stack = jnp.concatenate([local_grads[4], local_grads[5][None, :]], axis=0)
    summed = lax.psum((gain_slot, head_slot, chan_slot, shared_stack), ("dp", "row", "col"))
    gain_total = lax.dynamic_index_in_dim(summed[0], row_index, 0, keepdims=False)
    head_total = lax.dynamic_index_in_dim(summed[1], col_index, 1, keepdims=False)
    chan_total = lax.dynamic_index_in_dim(summed[2], col_index, 1, keepdims=False)
    stack_total = summed[3]
    return (
        block_output,
        input_grad,
        gain_total,
        inproj_total,
        shared_total,
        steps_total,
        outproj_total,
        chan_total[:tap_count],
        chan_total[tap_count],
        stack_total[:tap_count],
        stack_total[tap_count],
        head_total[0],
        head_total[1],
        head_total[2],
        chan_total[tap_count + 1],
    )


def solution(mesh):
    return jax.shard_map(
        per_device,
        mesh=mesh,
        in_specs=(
            P(("dp", "col"), None),
            P(("dp", "col"), "row"),
            P(),
            P(),
            P("row"),
            P("row", None, "col"),
            P("row", None),
            P("row", "col"),
            P("col", "row"),
            P(None, "col"),
            P("col"),
            P(),
            P(),
            P("col"),
            P("col"),
            P("col"),
            P("col"),
        ),
        out_specs=(
            P(("dp", "col"), "row"),
            P(("dp", "col"), "row"),
            P("row"),
            P("row", None, "col"),
            P("row", None),
            P("row", "col"),
            P("col", "row"),
            P(None, "col"),
            P("col"),
            P(),
            P(),
            P("col"),
            P("col"),
            P("col"),
            P("col"),
        ),
        check_vma=False,
    )
```

profile of v0, /device:TPU:0, one launch (start us, length us, event | category | flops | bytes accessed | tf_op | source)
XLA Modules:
  0.0 1226.2 jit_solution(14746132511163028913)
XLA Ops:
  12.6 12.3 %copy.74 = bf16[160,8,2,2560]{3,1,2,0:T(8,128)(2,1)} copy(bf16[160,8,2,2560]{3,2,1,0:T(2,128)(2,1)} %bitcast.83) | data formatting | bytes 26214400
  25.1 13.7 %all-gather.9.cloned.1.call-done = bf16[512,1280]{1,0:T(8,128)(2,1)} async-done(((bf16[256,1280]{1,0:T(8,128)(2,1)}), bf16[512,1280]{1,0:T(8,128)(2,1)}) %all-gather.9.cloned.1.call-update) | async-done | bytes 1310736 | tf_op jit(solution)/shard_map/all_gather | solution.py:142
  41.8 12.3 %fusion.106 = f32[512,5120]{1,0:T(8,128)} fusion(bf16[512,1280]{1,0:T(8,128)(2,1)S(1)} %copy-done.17, bf16[1280,5120]{1,0:T(8,128)(2,1)} %bitcast.84), kind=kOutput, calls=%fused_computation.194 | convolution fusion | flops 6710886400 | bytes 24903680 | tf_op jit(solution)/shard_map/dot_general | solution.py:146
  54.2 10.5 all-gather.13.cloned.1.call-done
  64.7 9.2 fusion.108
  83.8 14.8 %reduce-scatter.12.cloned.1.call-done = f32[256,5120]{1,0:T(8,128)} async-done(((f32[512,5120]{1,0:T(8,128)}), f32[256,5120]{1,0:T(8,128)}) %reduce-scatter.12.cloned.1.call-update) | async-done | bytes 5242896 | tf_op jit(solution)/shard_map/reduce_scatter | solution.py:145
  110.1 15.6 %fusion.33 = f32[256,40,64]{0,2,1:T(8,128)} fusion(f32[256,40,64]{0,2,1:T(8,128)} %bitcast.88, f32[256,40]{0,1:T(8,128)S(1)} %compare_select_fusion.2, f32[256,256]{1,0:T(8,128)} %convolution_select_fusion, f32[256,40]{0,1:T(8,128)S(1)} %fusion.64, pred[256,256]{1,0:T(8,128)(4,1)S(1)} %fusion.65, f32[256]{0:T(256)S(1)} %get-tuple-element.145, ...), kind=kOutput, calls=%fused_computation.49 | convolution fusion | flops 2025717760 | bytes 5653664 | tf_op jit(solution)/shard_map/jvp(tsh,shp->thp)/dot_general | solution.py:53
  154.2 11.6 bitcast_add_fusion
  182.7 18.6 %fusion.8 = (f32[256,40]{0,1:T(8,128)}, f32[256,40]{0,1:T(8,128)}, f32[256,40]{0,1:T(8,128)}, f32[256,256]{1,0:T(8,128)S(1)}) fusion(f32[256,40]{0,1:T(8,128)} %copy-done.31, f32[256,256]{1,0:T(8,128)} %convolution_select_fusion, f32[256,40]{0,1:T(8,128)} %copy-done.66, pred[256,256]{1,0:T(8,128)(4,1)S(1)} %fusion.65, f32[256,40,64]{0,2,1:T(8,128)S(1)} %bitcast.89, ...), kind=kOutput, calls=%fused_computation.15 | convolution fusion | flops 2047903744 | bytes 6038528 | tf_op jit(solution)/shard_map/transpose(jvp(tsh,shp->thp))/dot_general | solution.py:53
  236.7 55.0 %reduce-scatter.28.cloned.1.call-done = bf16[160,296]{1,0:T(8,128)(2,1)} async-done(((bf16[1280,296]{1,0:T(8,128)(2,1)}), bf16[160,296]{1,0:T(8,128)(2,1)}) %reduce-scatter.28.cloned.1.call-update) | async-done | bytes 94736
  293.5 13.9 %fusion.9 = f32[512,1280]{1,0:T(8,128)} fusion(bf16[1280,5120]{1,0:T(8,128)(2,1)} %bitcast.85, bf16[512,2560]{1,0:T(8,128)(2,1)} %all-gather.17.cloned.1.call-done, bf16[512,2560]{1,0:T(8,128)(2,1)} %all-gather.15.cloned.1.call-done), kind=kOutput, calls=%fused_computation.16 | convolution fusion | flops 6721372160 | bytes 20971520 | tf_op jit(solution)/shard_map/dot_general | solution.py:220
  321.2 95.2 %reduce-scatter.24.cloned.1.call-done = bf16[160,2560]{1,0:T(8,128)(2,1)} async-done(((bf16[1280,2560]{1,0:T(8,128)(2,1)}), bf16[160,2560]{1,0:T(8,128)(2,1)}) %reduce-scatter.24.cloned.1.call-update) | async-done | bytes 819216 | tf_op jit(solution)/shard_map/reduce_scatter | solution.py:59
  416.4 124.8 %reduce-scatter.22.cloned.1.call-done = bf16[160,2560]{1,0:T(8,128)(2,1)} async-done(((bf16[1280,2560]{1,0:T(8,128)(2,1)}), bf16[160,2560]{1,0:T(8,128)(2,1)}) %reduce-scatter.22.cloned.1.call-update) | async-done | bytes 819216 | tf_op jit(solution)/shard_map/reduce_scatter | solution.py:59
  541.3 124.2 %reduce-scatter.26.cloned.1.call-done = bf16[320,1280]{1,0:T(8,128)(2,1)} async-done(((bf16[2560,1280]{1,0:T(8,128)(2,1)}), bf16[320,1280]{1,0:T(8,128)(2,1)}) %reduce-scatter.26.cloned.1.call-update) | async-done | bytes 819216 | tf_op jit(solution)/shard_map/reduce_scatter | solution.py:59
  665.9 127.6 %all-reduce.32.cloned.1.call-done = f32[6,2,2560]{2,0,1:T(8,128)} async-done(((f32[6,2,2560]{2,0,1:T(8,128)}), f32[6,2,2560]{2,0,1:T(8,128)}) %all-reduce.32.cloned.1.call-update) | async-done | bytes 122896 | tf_op jit(solution)/shard_map/psum | solution.py:265
  796.7 23.0 %all-reduce.30.cloned.1.call-done = bf16[160,256]{0,1:T(8,128)(2,1)} async-done(((bf16[160,256]{0,1:T(8,128)(2,1)}), bf16[160,256]{0,1:T(8,128)(2,1)}) %all-reduce.30.cloned.1.call-update) | async-done | bytes 81936 | tf_op jit(solution)/shard_map/psum | solution.py:62
  820.8 33.0 %all_gather.38 = bf16[1280,296]{1,0:T(8,128)(2,1)S(1)} all-gather(bf16[160,296]{1,0:T(8,128)(2,1)S(1)} %copy.67), channel_id=1, replica_groups=mesh['dp'=8,'row'=2,'col'=2] {'dp'}, dimensions={0}, use_global_device_ids=true | all-gather | bytes 852480 | tf_op jit(solution)/shard_map/all_gather | solution.py:64
  862.1 40.3 %all-reduce.26 = (f32[2,1280]{1,0:T(2,128)S(1)}, f32[5,256]{1,0:T(8,128)S(1)}, f32[3,2,40]{2,1,0:T(2,128)S(1)}) all-reduce(f32[2,1280]{1,0:T(2,128)S(1)} %broadcast_multiply_fusion.7, f32[5,256]{1,0:T(8,128)S(1)} %pad_maximum_fusion.6, ...), channel_id=1, replica_groups=mesh['dp'=8,'row'=2,'col'=2] {'dp','row','col'}, use_global_device_ids=true, to_apply=%region_20.21 | all-reduce | flops 4080 | bytes 32640 | tf_op jit(solution)/shard_map/psum | solution.py:265
  910.2 94.8 %all-gather.21.cloned.1.call-done = bf16[1280,2560]{1,0:T(8,128)(2,1)} async-done(((bf16[160,2560]{1,0:T(8,128)(2,1)}), bf16[1280,2560]{1,0:T(8,128)(2,1)}) %all-gather.21.cloned.1.call-update) | async-done | bytes 6553616 | tf_op jit(solution)/shard_map/all_gather | solution.py:64
  1005.0 102.7 %all-gather.19.cloned.1.call-done = bf16[1280,2560]{1,0:T(8,128)(2,1)} async-done(((bf16[160,2560]{1,0:T(8,128)(2,1)}), bf16[1280,2560]{1,0:T(8,128)(2,1)}) %all-gather.19.cloned.1.call-update) | async-done | bytes 6553616 | tf_op jit(solution)/shard_map/all_gather | solution.py:64
  1107.7 14.4 %maximum_convert_fusion = f32[1280,2,2560]{2,0,1:T(8,128)} fusion(bf16[1280,1,2560]{2,0,1:T(8,128)(2,1)} %bitcast.86, bf16[1280,1,2560]{2,0,1:T(8,128)(2,1)} %bitcast.87), kind=kLoop, calls=%fused_computation | loop fusion | flops 13107200 | bytes 39321600 | tf_op jit(solution)/shard_map/convert_element_type | solution.py:248
  1122.1 43.6 %copy.68 = f32[1280,2,2560]{2,1,0:T(2,128)} copy(f32[1280,2,2560]{2,0,1:T(8,128)} %maximum_convert_fusion) | data formatting | bytes 52428800
  1165.7 44.9 %all-gather.23.cloned.1.call-done = bf16[2560,1280]{1,0:T(8,128)(2,1)} async-done(((bf16[320,1280]{1,0:T(8,128)(2,1)}), bf16[2560,1280]{1,0:T(8,128)(2,1)}) %all-gather.23.cloned.1.call-update) | async-done | bytes 6553616 | tf_op jit(solution)/shard_map/all_gather | solution.py:64
  1210.6 8.8 convert_element_type.112
  (291 shorter events, 146.2 us)
Async XLA Ops:
  7.2 31.7 %all-gather.9.cloned.1.call-start = ((), (), s32[]{:S(2)}) async-start(), calls=%async_computation.9 | async-start | bytes 1966080 | tf_op jit(solution)/shard_map/all_gather | solution.py:142
  11.8 52.9 %all-gather.13.cloned.1.call-start = ((), (), s32[]{:S(2)}) async-start(), calls=%async_computation.14 | async-start | bytes 1966080 | tf_op jit(solution)/shard_map/all_gather | solution.py:191
  12.5 63.1 %reduce-scatter.14.cloned.1.call-start = ((), (), s32[]{:S(2)}) async-start(), calls=%async_computation.11 | async-start | bytes 909312 | tf_op jit(solution)/shard_map/reduce_scatter | solution.py:151
  41.8 56.8 %reduce-scatter.12.cloned.1.call-start = ((), (), s32[]{:S(2)}) async-start(), calls=%async_computation.10 | async-start | bytes 15728640 | tf_op jit(solution)/shard_map/reduce_scatter | solution.py:145
  54.2 82.6 %reduce-scatter.18.cloned.1.call-start = ((), (), s32[]{:S(2)}) async-start(), calls=%async_computation.15 | async-start | bytes 7864320 | tf_op jit(solution)/shard_map/reduce_scatter | solution.py:193
  74.0 136.6 %all-gather.17.cloned.1.call-start = ((), (), s32[]{:S(2)}) async-start(), calls=%async_computation.17 | async-start | bytes 3932160 | tf_op jit(solution)/shard_map/all_gather | solution.py:217
  75.2 94.0 %copy-start.37 = (f32[256]{0:T(256)}, f32[256]{0:T(256)S(1)}, u32[]{:S(2)}) copy-start(f32[256]{0:T(256)S(1)} %get-tuple-element.142) | copy-start | bytes 3076
  75.2 98.1 %copy-start.33 = (f32[256]{0:T(256)}, f32[256]{0:T(256)S(1)}, u32[]{:S(2)}) copy-start(f32[256]{0:T(256)S(1)} %get-tuple-element.140) | copy-start | bytes 3076
  75.2 98.1 %copy-start.35 = (f32[256]{0:T(256)}, f32[256]{0:T(256)S(1)}, u32[]{:S(2)}) copy-start(f32[256]{0:T(256)S(1)} %get-tuple-element.141) | copy-start | bytes 3076
  180.9 37.0 %all-gather.15.cloned.1.call-start = ((), (), s32[]{:S(2)}) async-start(), calls=%async_computation.16 | async-start | bytes 3932160 | tf_op jit(solution)/shard_map/all_gather | solution.py:210
  181.7 44.2 %all-gather.11.cloned.1.call-start = ((), (), s32[]{:S(2)}) async-start(), calls=%async_computation.12 | async-start | bytes 3932160 | tf_op jit(solution)/shard_map/all_gather | solution.py:182
  202.0 89.6 %reduce-scatter.28.cloned.1.call-start = ((), (), s32[]{:S(2)}) async-start(), calls=%async_computation.27 | async-start | bytes 1105920
  210.5 205.8 %reduce-scatter.24.cloned.1.call-start = ((), (), s32[]{:S(2)}) async-start(), calls=%async_computation.21 | async-start | bytes 7372800 | tf_op jit(solution)/shard_map/reduce_scatter | solution.py:59
  217.9 323.3 %reduce-scatter.22.cloned.1.call-start = ((), (), s32[]{:S(2)}) async-start(), calls=%async_computation.19 | async-start | bytes 7372800 | tf_op jit(solution)/shard_map/reduce_scatter | solution.py:59
  225.6 439.9 %reduce-scatter.26.cloned.1.call-start = ((), (), s32[]{:S(2)}) async-start(), calls=%async_computation.24 | async-start | bytes 7372800 | tf_op jit(solution)/shard_map/reduce_scatter | solution.py:59
  235.0 558.5 %all-reduce.32.cloned.1.call-start = ((), (), s32[]{:S(2)}) async-start(), calls=%async_computation.26 | async-start | bytes 327680 | tf_op jit(solution)/shard_map/psum | solution.py:265
  236.6 583.1 %all-reduce.30.cloned.1.call-start = ((), (), s32[]{:S(2)}) async-start(), calls=%async_computation.23 | async-start | bytes 262144 | tf_op jit(solution)/shard_map/psum | solution.py:62
  293.4 566.7 %reduce-scatter.20.cloned.1.call-start = ((), (), s32[]{:S(2)}) async-start(), calls=%async_computation.18 | async-start | bytes 3932160 | tf_op jit(solution)/shard_map/reduce_scatter | solution.py:219
  311.5 595.6 %reduce-scatter.16.cloned.1.call-start = ((), (), s32[]{:S(2)}) async-start(), calls=%async_computation.13 | async-start | bytes 3932160 | tf_op jit(solution)/shard_map/reduce_scatter | solution.py:184
  321.1 344.6 %copy-start.63 = (f32[40]{0:T(128)S(1)}, f32[40]{0:T(128)}, u32[]{:S(2)}) copy-start(f32[40]{0:T(128)} %param.30) | copy-start | bytes 484
  321.1 475.5 %slice-start.2 = ((bf16[160,296]{1,0:T(8,128)(2,1)}), bf16[160,40]{1,0:T(8,128)(2,1)S(1)}, s32[]{:S(2)}) async-start(bf16[160,296]{1,0:T(8,128)(2,1)} %reduce-scatter.28.cloned.1.call-done), calls=%async_computation.30 | async-start | bytes 81920 | tf_op jit(solution)/shard_map/slice | solution.py:63
  321.2 683.9 %all-gather.21.cloned.1.call-start = ((), (), s32[]{:S(2)}) async-start(), calls=%async_computation.22 | async-start | bytes 7372800 | tf_op jit(solution)/shard_map/all_gather | solution.py:64
  416.4 691.4 %all-gather.19.cloned.1.call-start = ((), (), s32[]{:S(2)}) async-start(), calls=%async_computation.20 | async-start | bytes 7372800 | tf_op jit(solution)/shard_map/all_gather | solution.py:64
  541.2 669.3 %all-gather.23.cloned.1.call-start = ((), (), s32[]{:S(2)}) async-start(), calls=%async_computation.25 | async-start | bytes 7372800 | tf_op jit(solution)/shard_map/all_gather | solution.py:64
  (65 other events, 773.5 us)
Sparse Core Ops, SparseCore 0:
  11.9 26.9 all-gather.8
  40.4 24.2 all-gather.12
  67.6 8.0 reduce-scatter.13
  78.4 20.1 reduce-scatter.11
  100.8 14.4 reduce-scatter.17
  181.1 12.5 all-gather.16
  195.9 12.6 all-gather.14
  210.8 12.5 all-gather.10
  227.1 64.4 reduce-scatter.27
  295.7 120.6 reduce-scatter.23
  420.4 120.7 reduce-scatter.21
  544.7 120.7 reduce-scatter.25
  672.5 120.9 all-reduce.31
  796.3 23.4 all-reduce.29
  822.5 37.5 reduce-scatter.19
  862.2 38.2 reduce-scatter.15
  902.8 102.1 all-gather.20
  1007.3 100.3 all-gather.18
  1110.1 100.3 all-gather.22
where the time goes:
time: 1230 us
  waiting for transfers between devices  837 us (68%)
  matrix products  124 us (10%)
  local copies, waits for them, and re-layouts  92.5 us (8%)
  blocking collectives  87.9 us (7%)
  other arithmetic  67.7 us (6%)
  between operations  15.3 us (1%)
    reduce_scatter x3, waiting for transfers between devices, sum_rows_over_dp(): lax.psum_scatter(part.astype(jnp.bfloat16), 'dp', scatter_dimension=0, ti...  344 us
    all_gather x3, waiting for transfers between devices, sum_rows_over_dp(): return lax.all_gather(piece, 'dp', axis=0, tiled=True)  242 us
    psum x1, waiting for transfers between devices, per_device(): lax.psum((gain_slot, head_slot, chan_slot, shared_stack), ('dp', 'row', '...  128 us
    unnamed x145, local copies, waits for them, and re-layouts  68.9 us
    unnamed x20, waiting for transfers between devices  56.6 us
    dot_general x3, matrix products, mix_bucket(): within = jnp.einsum('tsh,shp->thp', weights, values, precision=PRECISE)  45.7 us
    psum x1, blocking collectives, per_device(): lax.psum((gain_slot, head_slot, chan_slot, shared_stack), ('dp', 'row', '...  40.3 us
    all_gather x1, blocking collectives, sum_rows_over_dp(): return lax.all_gather(piece, 'dp', axis=0, tiled=True)  33 us
  transfers between devices with their start and end apart: 19, of which 14 were waited for; matrix products, arithmetic and copies ran while one was open for 18% of the time, Pallas kernels for 0%

commit v1 on v0

--- a/solution.py
+++ b/solution.py
@@ -8,6 +8,24 @@
 CAP = 256
 EPSILON = 1e-05
 PRECISE = lax.Precision.HIGHEST
+
+
+def collect(shard, axis, dim):
+    ways, here, step = (lax.axis_size(axis), lax.axis_index(axis), shard.shape[dim])
+    shape = [n * ways if d == dim else n for d, n in enumerate(shard.shape)]
+    full = lax.dynamic_update_slice_in_dim(
+        jnp.zeros(shape, shard.dtype), shard, here * step, axis=dim
+    )
+    going_up = going_down = shard
+    for far in range(1, ways // 2 + 1):
+        going_up = lax.ppermute(going_up, axis, [(d, (d + 1) % ways) for d in range(ways)])
+        full = lax.dynamic_update_slice_in_dim(full, going_up, (here - far) % ways * step, axis=dim)
+        if 2 * far < ways:
+            going_down = lax.ppermute(going_down, axis, [(d, (d - 1) % ways) for d in range(ways)])
+            full = lax.dynamic_update_slice_in_dim(
+                full, going_down, (here + far) % ways * step, axis=dim
+            )
+    return full
 
 
 def layout(seq_lengths, seq_owner, bucket, capacity):
@@ -61,7 +79,7 @@
         own = piece.shape[1] - shared_cols
         tail = lax.psum(piece[:, own:].astype(jnp.float32), "col").astype(jnp.bfloat16)
         piece = jnp.concatenate([piece[:, :own], tail], axis=1)
-    return lax.all_gather(piece, "dp", axis=0, tiled=True)
+    return collect(piece, "dp", 0)
 
 
 def mixer_local(

time: 1230 us -> 1320 us (1.073)
  starting transfers between devices: 1.53 us -> 59.8 us
  local copies, waits for them, and re-layouts: 92.5 us -> 126 us
  blocking collectives: 87.9 us -> 55 us
  other arithmetic: 67.7 us -> 95.6 us
    all_gather x3 -> x0, waiting for transfers between devices: 242 us -> none  [sum_rows_over_dp(): return lax.all_gather(piece, 'dp', axis=0, tiled=True)]
    ppermute x0 -> x28, waiting for transfers between devices: none -> 242 us  [the longest x16 123 us: collect(): lax.ppermute(going_up, axis, [(d, (d + 1) % ways) for d in range(ways)])]
    dynamic_update_slice x0 -> x32, local copies, waits for them, and re-layouts: none -> 59.8 us  [the longest x16 30 us: collect(): lax.dynamic_update_slice_in_dim(full, going_up, (here - far) % ways * ste...]
    ppermute x0 -> x28, starting transfers between devices: none -> 58.8 us  [the longest x12 42.1 us: collect(): lax.ppermute(going_down, axis, [(d, (d - 1) % ways) for d in range(ways)])]
    unnamed x145 -> x158, local copies, waits for them, and re-layouts: 68.9 us -> 25 us
    psum x1, waiting for transfers between devices: 128 us -> 88.5 us  [per_device(): lax.psum((gain_slot, head_slot, chan_slot, shared_stack), ('dp', 'row', '...]
    all_gather x1 -> x0, blocking collectives: 33 us -> none  [sum_rows_over_dp(): return lax.all_gather(piece, 'dp', axis=0, tiled=True)]
    reduce_scatter x3, waiting for transfers between devices: 344 us -> 375 us  [sum_rows_over_dp(): lax.psum_scatter(part.astype(jnp.bfloat16), 'dp', scatter_dimension=0, ti...]
  transfers between devices with their start and end apart: 19 -> 44, of which waited for: 14 -> 27; matrix products, arithmetic and copies ran while one was open for 18% -> 18% of each run, Pallas kernels for 0% -> 0%
where the time goes in v1:
time: 1320 us; the launch traced here: 1310 us
  waiting for transfers between devices  841 us (64%)
  local copies, waits for them, and re-layouts  126 us (10%)
  matrix products  119 us (9%)
  other arithmetic  95.6 us (7%)
  starting transfers between devices  59.8 us (5%)
  blocking collectives  55 us (4%)
  between operations  15.6 us (1%)
    reduce_scatter x3, waiting for transfers between devices, sum_rows_over_dp(): lax.psum_scatter(part.astype(jnp.bfloat16), 'dp', scatter_dimension=0, ti...  375 us
    ppermute x16, waiting for transfers between devices, collect(): lax.ppermute(going_up, axis, [(d, (d + 1) % ways) for d in range(ways)])  123 us
    ppermute x12, waiting for transfers between devices, collect(): lax.ppermute(going_down, axis, [(d, (d - 1) % ways) for d in range(ways)])  118 us
    psum x1, waiting for transfers between devices, per_device(): lax.psum((gain_slot, head_slot, chan_slot, shared_stack), ('dp', 'row', '...  88.5 us
    unnamed x17, waiting for transfers between devices  56.8 us
    dot_general x3, matrix products, mix_bucket(): within = jnp.einsum('tsh,shp->thp', weights, values, precision=PRECISE)  43.7 us
    ppermute x12, starting transfers between devices, collect(): lax.ppermute(going_down, axis, [(d, (d - 1) % ways) for d in range(ways)])  42.1 us
    psum x1, blocking collectives, per_device(): lax.psum((gain_slot, head_slot, chan_slot, shared_stack), ('dp', 'row', '...  40 us
  transfers between devices with their start and end apart: 44, of which 27 were waited for; matrix products, arithmetic and copies ran while one was open for 18% of the time, Pallas kernels for 0%

profile of v1, /device:TPU:0, one launch (start us, length us, event | category | flops | bytes accessed | tf_op | source)
XLA Modules:
  0.0 1311.6 jit_solution(12672848442774705218)
XLA Ops:
  25.1 13.7 %all-gather.6.cloned.1.call-done = bf16[512,1280]{1,0:T(8,128)(2,1)} async-done(((bf16[256,1280]{1,0:T(8,128)(2,1)}), bf16[512,1280]{1,0:T(8,128)(2,1)}) %all-gather.6.cloned.1.call-update) | async-done | bytes 1310736 | tf_op jit(solution)/shard_map/all_gather | solution.py:160
  84.7 13.9 %reduce-scatter.12.cloned.1.call-done = f32[256,5120]{1,0:T(8,128)} async-done(((f32[512,5120]{1,0:T(8,128)}), f32[256,5120]{1,0:T(8,128)}) %reduce-scatter.12.cloned.1.call-update) | async-done | bytes 5242896 | tf_op jit(solution)/shard_map/reduce_scatter | solution.py:163
  110.2 15.7 %fusion.33 = f32[256,40,64]{0,2,1:T(8,128)} fusion(f32[256,40,64]{0,2,1:T(8,128)} %bitcast.101, f32[256,40]{0,1:T(8,128)} %copy-done.33, f32[256,256]{1,0:T(8,128)} %convolution_select_fusion, f32[256,40]{0,1:T(8,128)} %fusion.64, pred[256,256]{1,0:T(8,128)(4,1)S(1)} %fusion.65, f32[256]{0:T(256)S(1)} %copy-done.55, f32[40]{0:T(128)S(1)} %copy-done.65), kind=kOutput, calls=%fused_computation.49 | convolution fusion | flops 2025717760 | bytes 5653664 | tf_op jit(solution)/shard_map/jvp(tsh,shp->thp)/dot_general | solution.py:71
  167.6 16.3 %fusion.8 = (f32[256,40]{0,1:T(8,128)S(1)}, f32[256,40]{0,1:T(8,128)S(1)}, f32[256,40]{0,1:T(8,128)S(1)}, f32[256,256]{1,0:T(8,128)S(1)}) fusion(f32[256,40]{0,1:T(8,128)S(1)} %copy-done.34, f32[256,256]{1,0:T(8,128)S(1)} %copy-done.69, f32[256,40]{0,1:T(8,128)S(1)} %copy-done.73, pred[256,256]{1,0:T(8,128)(4,1)S(1)} %fusion.65, ...), kind=kOutput, calls=%fused_computation.15 | convolution fusion | flops 2047903744 | bytes 6038528 | tf_op jit(solution)/shard_map/transpose(jvp(tsh,shp->thp))/dot_general | solution.py:71
  215.5 54.6 %reduce-scatter.28.cloned.1.call-done = bf16[160,296]{1,0:T(8,128)(2,1)} async-done(((bf16[1280,296]{1,0:T(8,128)(2,1)}), bf16[160,296]{1,0:T(8,128)(2,1)}) %reduce-scatter.28.cloned.1.call-update) | async-done | bytes 94736
  282.6 14.7 %all-gather.12.cloned.1.call-done = bf16[512,2560]{1,0:T(8,128)(2,1)} async-done(((bf16[256,2560]{1,0:T(8,128)(2,1)}), bf16[512,2560]{1,0:T(8,128)(2,1)}) %all-gather.12.cloned.1.call-update) | async-done | bytes 2621456 | tf_op jit(solution)/shard_map/all_gather | solution.py:228
  376.9 88.5 %all-reduce.32.cloned.1.call-done = f32[6,2,2560]{2,0,1:T(8,128)} async-done(((f32[6,2,2560]{2,0,1:T(8,128)}), f32[6,2,2560]{2,0,1:T(8,128)}) %all-reduce.32.cloned.1.call-update) | async-done | bytes 122896 | tf_op jit(solution)/shard_map/psum | solution.py:283
  491.5 15.7 %reduce-scatter.20.cloned.1.call-done = f32[256,1280]{1,0:T(8,128)} async-done(((f32[512,1280]{1,0:T(8,128)}), f32[256,1280]{1,0:T(8,128)}) %reduce-scatter.20.cloned.1.call-update) | async-done | bytes 1310736 | tf_op jit(solution)/shard_map/reduce_scatter | solution.py:237
  509.1 40.0 %all-reduce.26 = (f32[2,1280]{1,0:T(2,128)S(1)}, f32[5,256]{1,0:T(8,128)S(1)}, f32[3,2,40]{2,1,0:T(2,128)S(1)}) all-reduce(f32[2,1280]{1,0:T(2,128)S(1)} %broadcast_multiply_fusion.7, f32[5,256]{1,0:T(8,128)S(1)} %pad_maximum_fusion.6, ...), channel_id=1, replica_groups=mesh['dp'=8,'row'=2,'col'=2] {'dp','row','col'}, use_global_device_ids=true, to_apply=%region_20.21 | all-reduce | flops 4080 | bytes 32640 | tf_op jit(solution)/shard_map/psum | solution.py:283
  557.2 116.3 %reduce-scatter.24.cloned.1.call-done = bf16[160,2560]{1,0:T(8,128)(2,1)} async-done(((bf16[1280,2560]{1,0:T(8,128)(2,1)}), bf16[160,2560]{1,0:T(8,128)(2,1)}) %reduce-scatter.24.cloned.1.call-update) | async-done | bytes 819216 | tf_op jit(solution)/shard_map/reduce_scatter | solution.py:77
  678.3 134.7 %reduce-scatter.22.cloned.1.call-done = bf16[160,2560]{1,0:T(8,128)(2,1)} async-done(((bf16[1280,2560]{1,0:T(8,128)(2,1)}), bf16[160,2560]{1,0:T(8,128)(2,1)}) %reduce-scatter.22.cloned.1.call-update) | async-done | bytes 819216 | tf_op jit(solution)/shard_map/reduce_scatter | solution.py:77
  828.3 124.2 %reduce-scatter.26.cloned.1.call-done = bf16[320,1280]{1,0:T(8,128)(2,1)} async-done(((bf16[2560,1280]{1,0:T(8,128)(2,1)}), bf16[320,1280]{1,0:T(8,128)(2,1)}) %reduce-scatter.26.cloned.1.call-update) | async-done | bytes 819216 | tf_op jit(solution)/shard_map/reduce_scatter | solution.py:77
  982.5 25.8 %collective-permute-done.21 = bf16[320,1280]{1,0:T(8,128)(2,1)S(1)} collective-permute-done((bf16[320,1280]{1,0:T(8,128)(2,1)}, bf16[320,1280]{1,0:T(8,128)(2,1)S(1)}, u32[]{:S(2)}, u32[]{:S(2)}) %collective-permute-start.21) | collective-permute-done | bytes 819232 | tf_op jit(solution)/shard_map/ppermute | solution.py:21
  1013.9 13.7 %collective-permute-done.22 = bf16[320,1280]{1,0:T(8,128)(2,1)S(1)} collective-permute-done((bf16[320,1280]{1,0:T(8,128)(2,1)S(1)}, bf16[320,1280]{1,0:T(8,128)(2,1)S(1)}, u32[]{:S(2)}, u32[]{:S(2)}) %collective-permute-start.22) | collective-permute-done | bytes 819232 | tf_op jit(solution)/shard_map/ppermute | solution.py:24
  1028.6 14.8 %collective-permute-done.9 = bf16[160,2560]{1,0:T(8,128)(2,1)S(1)} collective-permute-done((bf16[160,2560]{1,0:T(8,128)(2,1)}, bf16[160,2560]{1,0:T(8,128)(2,1)S(1)}, u32[]{:S(2)}, u32[]{:S(2)}) %collective-permute-start.9) | collective-permute-done | bytes 819232 | tf_op jit(solution)/shard_map/ppermute | solution.py:21
  1049.2 13.6 %collective-permute-done.10 = bf16[160,2560]{1,0:T(8,128)(2,1)S(1)} collective-permute-done((bf16[160,2560]{1,0:T(8,128)(2,1)S(1)}, bf16[160,2560]{1,0:T(8,128)(2,1)S(1)}, u32[]{:S(2)}, u32[]{:S(2)}) %collective-permute-start.10) | collective-permute-done | bytes 819232 | tf_op jit(solution)/shard_map/ppermute | solution.py:24
  1083.4 14.5 %collective-permute-done.3 = bf16[160,2560]{1,0:T(8,128)(2,1)S(1)} collective-permute-done((bf16[160,2560]{1,0:T(8,128)(2,1)S(1)}, bf16[160,2560]{1,0:T(8,128)(2,1)S(1)}, u32[]{:S(2)}, u32[]{:S(2)}) %collective-permute-start.3) | collective-permute-done | bytes 819232 | tf_op jit(solution)/shard_map/ppermute | solution.py:24
  1097.9 15.6 %collective-permute-done.23 = bf16[320,1280]{1,0:T(8,128)(2,1)S(1)} collective-permute-done((bf16[320,1280]{1,0:T(8,128)(2,1)S(1)}, bf16[320,1280]{1,0:T(8,128)(2,1)S(1)}, u32[]{:S(2)}, u32[]{:S(2)}) %collective-permute-start.23) | collective-permute-done | bytes 819232 | tf_op jit(solution)/shard_map/ppermute | solution.py:21
  1119.3 13.7 %collective-permute-done.24 = bf16[320,1280]{1,0:T(8,128)(2,1)S(1)} collective-permute-done((bf16[320,1280]{1,0:T(8,128)(2,1)S(1)}, bf16[320,1280]{1,0:T(8,128)(2,1)S(1)}, u32[]{:S(2)}, u32[]{:S(2)}) %collective-permute-start.24) | collective-permute-done | bytes 819232 | tf_op jit(solution)/shard_map/ppermute | solution.py:24
  1133.9 14.7 %collective-permute-done.11 = bf16[160,2560]{1,0:T(8,128)(2,1)S(1)} collective-permute-done((bf16[160,2560]{1,0:T(8,128)(2,1)S(1)}, bf16[160,2560]{1,0:T(8,128)(2,1)S(1)}, u32[]{:S(2)}, u32[]{:S(2)}) %collective-permute-start.11) | collective-permute-done | bytes 819232 | tf_op jit(solution)/shard_map/ppermute | solution.py:21
  1154.6 13.5 %collective-permute-done.12 = bf16[160,2560]{1,0:T(8,128)(2,1)S(1)} collective-permute-done((bf16[160,2560]{1,0:T(8,128)(2,1)S(1)}, bf16[160,2560]{1,0:T(8,128)(2,1)S(1)}, u32[]{:S(2)}, u32[]{:S(2)}) %collective-permute-start.12) | collective-permute-done | bytes 819232 | tf_op jit(solution)/shard_map/ppermute | solution.py:24
  1168.1 15.7 %collective-permute-done.4 = bf16[160,2560]{1,0:T(8,128)(2,1)S(1)} collective-permute-done((bf16[160,2560]{1,0:T(8,128)(2,1)S(1)}, bf16[160,2560]{1,0:T(8,128)(2,1)S(1)}, u32[]{:S(2)}, u32[]{:S(2)}) %collective-permute-start.4) | collective-permute-done | bytes 819232 | tf_op jit(solution)/shard_map/ppermute | solution.py:21
  1206.4 49.4 %collective-permute-done.26 = bf16[320,1280]{1,0:T(8,128)(2,1)S(1)} collective-permute-done((bf16[320,1280]{1,0:T(8,128)(2,1)S(1)}, bf16[320,1280]{1,0:T(8,128)(2,1)S(1)}, u32[]{:S(2)}, u32[]{:S(2)}) %collective-permute-start.26) | collective-permute-done | bytes 819232 | tf_op jit(solution)/shard_map/ppermute | solution.py:24
  1271.8 33.1 %maximum_convert_fusion = f32[1280,2,2560]{2,1,0:T(2,128)} fusion(bf16[1280,1,2560]{2,1,0:T(2,128)(2,1)} %copy_dynamic-update-slice_fusion, bf16[1280,1,2560]{2,1,0:T(2,128)(2,1)S(1)} %copy_dynamic-update-slice_fusion.8), kind=kLoop, calls=%fused_computation | loop fusion | flops 26214400 | bytes 39321600 | tf_op jit(solution)/shard_map/convert_element_type | solution.py:266
  (387 shorter events, 409.5 us)
Async XLA Ops:
  74.0 196.0 %reduce-scatter.28.cloned.1.call-start = ((), (), s32[]{:S(2)}) async-start(), calls=%async_computation.24 | async-start | bytes 1105920
  214.5 99.2 %all-gather.8.cloned.1.call-start = ((), (), s32[]{:S(2)}) async-start(), calls=%async_computation.12 | async-start | bytes 3932160 | tf_op jit(solution)/shard_map/all_gather | solution.py:200
  215.2 132.8 %all-reduce.30.cloned.1.call-start = ((), (), s32[]{:S(2)}) async-start(), calls=%async_computation.21 | async-start | bytes 262144 | tf_op jit(solution)/shard_map/psum | solution.py:80
  271.8 193.6 %all-reduce.32.cloned.1.call-start = ((), (), s32[]{:S(2)}) async-start(), calls=%async_computation.23 | async-start | bytes 327680 | tf_op jit(solution)/shard_map/psum | solution.py:283
  272.7 234.5 %reduce-scatter.20.cloned.1.call-start = ((), (), s32[]{:S(2)}) async-start(), calls=%async_computation.18 | async-start | bytes 3932160 | tf_op jit(solution)/shard_map/reduce_scatter | solution.py:237
  313.5 240.4 %reduce-scatter.16.cloned.1.call-start = ((), (), s32[]{:S(2)}) async-start(), calls=%async_computation.13 | async-start | bytes 3932160 | tf_op jit(solution)/shard_map/reduce_scatter | solution.py:202
  322.5 351.0 %reduce-scatter.24.cloned.1.call-start = ((), (), s32[]{:S(2)}) async-start(), calls=%async_computation.20 | async-start | bytes 7372800 | tf_op jit(solution)/shard_map/reduce_scatter | solution.py:77
  331.1 481.8 %reduce-scatter.22.cloned.1.call-start = ((), (), s32[]{:S(2)}) async-start(), calls=%async_computation.19 | async-start | bytes 7372800 | tf_op jit(solution)/shard_map/reduce_scatter | solution.py:77
  338.5 613.9 %reduce-scatter.26.cloned.1.call-start = ((), (), s32[]{:S(2)}) async-start(), calls=%async_computation.22 | async-start | bytes 7372800 | tf_op jit(solution)/shard_map/reduce_scatter | solution.py:77
  368.9 115.2 %collective-permute-start.19 = (bf16[160,296]{0,1:T(8,128)(2,1)S(1)}, bf16[160,296]{0,1:T(8,128)(2,1)S(1)}, u32[]{:S(2)}, u32[]{:S(2)}) collective-permute-start(bf16[160,296]{0,1:T(8,128)(2,1)S(1)} %collective-permute-done.17), channel_id=1, source_target_pairs={{0,28},{4,0},{8,4},{12,8},{16,12},{20,16},{24,20},{28,24},{1,29},{... | collective-permute-start | bytes 284168 | tf_op jit(solution)/shard_map/ppermute | solution.py:24
  376.3 110.7 %collective-permute-start.20 = (bf16[160,296]{0,1:T(8,128)(2,1)S(1)}, bf16[160,296]{0,1:T(8,128)(2,1)S(1)}, u32[]{:S(2)}, u32[]{:S(2)}) collective-permute-start(bf16[160,296]{0,1:T(8,128)(2,1)S(1)} %collective-permute-done.18), channel_id=1, source_target_pairs={{0,4},{4,8},{8,12},{12,16},{16,20},{20,24},{24,28},{28,0},{1,5},{5... | collective-permute-start | bytes 284168 | tf_op jit(solution)/shard_map/ppermute | solution.py:21
  673.5 293.4 %collective-permute-start.7 = (bf16[160,2560]{1,0:T(8,128)(2,1)}, bf16[160,2560]{1,0:T(8,128)(2,1)}, u32[]{:S(2)}, u32[]{:S(2)}) collective-permute-start(bf16[160,2560]{1,0:T(8,128)(2,1)} %reduce-scatter.24.cloned.1.call-done), channel_id=1, source_target_pairs={{0,4},{4,8},{8,12},{12,16},{16,20},{20,24},{24,28},{28,0},{1,5},{5... | collective-permute-start | bytes 2457608 | tf_op jit(solution)/shard_map/ppermute | solution.py:21
  675.0 298.8 %collective-permute-start.8 = (bf16[160,2560]{1,0:T(8,128)(2,1)}, bf16[160,2560]{1,0:T(8,128)(2,1)S(1)}, u32[]{:S(2)}, u32[]{:S(2)}) collective-permute-start(bf16[160,2560]{1,0:T(8,128)(2,1)} %reduce-scatter.24.cloned.1.call-done), channel_id=1, source_target_pairs={{0,28},{4,0},{8,4},{12,8},{16,12},{20,16},{24,20},{28,24},{1,29},{... | collective-permute-start | bytes 2457608 | tf_op jit(solution)/shard_map/ppermute | solution.py:24
  813.0 163.3 %collective-permute-start = (bf16[160,2560]{1,0:T(8,128)(2,1)}, bf16[160,2560]{1,0:T(8,128)(2,1)S(1)}, u32[]{:S(2)}, u32[]{:S(2)}) collective-permute-start(bf16[160,2560]{1,0:T(8,128)(2,1)} %reduce-scatter.22.cloned.1.call-done), channel_id=1, source_target_pairs={{0,4},{4,8},{8,12},{12,16},{16,20},{20,24},{24,28},{28,0},{1,5},{5... | collective-permute-start | bytes 2457608 | tf_op jit(solution)/shard_map/ppermute | solution.py:21
  814.4 168.0 %collective-permute-start.1 = (bf16[160,2560]{1,0:T(8,128)(2,1)}, bf16[160,2560]{1,0:T(8,128)(2,1)S(1)}, u32[]{:S(2)}, u32[]{:S(2)}) collective-permute-start(bf16[160,2560]{1,0:T(8,128)(2,1)} %reduce-scatter.22.cloned.1.call-done), channel_id=1, source_target_pairs={{0,28},{4,0},{8,4},{12,8},{16,12},{20,16},{24,20},{28,24},{1,29},{... | collective-permute-start | bytes 2457608 | tf_op jit(solution)/shard_map/ppermute | solution.py:24
  976.3 86.5 %collective-permute-start.10 = (bf16[160,2560]{1,0:T(8,128)(2,1)S(1)}, bf16[160,2560]{1,0:T(8,128)(2,1)S(1)}, u32[]{:S(2)}, u32[]{:S(2)}) collective-permute-start(bf16[160,2560]{1,0:T(8,128)(2,1)S(1)} %collective-permute-done.8), channel_id=1, source_target_pairs={{0,28},{4,0},{8,4},{12,8},{16,12},{20,16},{24,20},{28,24},{1,29},{... | collective-permute-start | bytes 2457608 | tf_op jit(solution)/shard_map/ppermute | solution.py:24
  982.4 96.1 %collective-permute-start.2 = (bf16[160,2560]{1,0:T(8,128)(2,1)S(1)}, bf16[160,2560]{1,0:T(8,128)(2,1)S(1)}, u32[]{:S(2)}, u32[]{:S(2)}) collective-permute-start(bf16[160,2560]{1,0:T(8,128)(2,1)S(1)} %collective-permute-done), channel_id=1, source_target_pairs={{0,4},{4,8},{8,12},{12,16},{16,20},{20,24},{24,28},{28,0},{1,5},{5... | collective-permute-start | bytes 2457608 | tf_op jit(solution)/shard_map/ppermute | solution.py:21
  1008.3 89.6 %collective-permute-start.3 = (bf16[160,2560]{1,0:T(8,128)(2,1)S(1)}, bf16[160,2560]{1,0:T(8,128)(2,1)S(1)}, u32[]{:S(2)}, u32[]{:S(2)}) collective-permute-start(bf16[160,2560]{1,0:T(8,128)(2,1)S(1)} %collective-permute-done.1), channel_id=1, source_target_pairs={{0,28},{4,0},{8,4},{12,8},{16,12},{20,16},{24,20},{28,24},{1,29},{... | collective-permute-start | bytes 2457608 | tf_op jit(solution)/shard_map/ppermute | solution.py:24
  1043.4 89.6 %collective-permute-start.24 = (bf16[320,1280]{1,0:T(8,128)(2,1)S(1)}, bf16[320,1280]{1,0:T(8,128)(2,1)S(1)}, u32[]{:S(2)}, u32[]{:S(2)}) collective-permute-start(bf16[320,1280]{1,0:T(8,128)(2,1)S(1)} %collective-permute-done.22), channel_id=1, source_target_pairs={{0,28},{4,0},{8,4},{12,8},{16,12},{20,16},{24,20},{28,24},{1,29},{... | collective-permute-start | bytes 2457608 | tf_op jit(solution)/shard_map/ppermute | solution.py:24
  1078.5 89.6 %collective-permute-start.12 = (bf16[160,2560]{1,0:T(8,128)(2,1)S(1)}, bf16[160,2560]{1,0:T(8,128)(2,1)S(1)}, u32[]{:S(2)}, u32[]{:S(2)}) collective-permute-start(bf16[160,2560]{1,0:T(8,128)(2,1)S(1)} %collective-permute-done.10), channel_id=1, source_target_pairs={{0,28},{4,0},{8,4},{12,8},{16,12},{20,16},{24,20},{28,24},{1,29},{... | collective-permute-start | bytes 2457608 | tf_op jit(solution)/shard_map/ppermute | solution.py:24
  1113.5 143.2 %collective-permute-start.5 = (bf16[160,2560]{1,0:T(8,128)(2,1)S(1)}, bf16[160,2560]{1,0:T(8,128)(2,1)S(1)}, u32[]{:S(2)}, u32[]{:S(2)}) collective-permute-start(bf16[160,2560]{1,0:T(8,128)(2,1)S(1)} %collective-permute-done.3), channel_id=1, source_target_pairs={{0,28},{4,0},{8,4},{12,8},{16,12},{20,16},{24,20},{28,24},{1,29},{... | collective-permute-start | bytes 2457608 | tf_op jit(solution)/shard_map/ppermute | solution.py:24
  1148.6 107.2 %collective-permute-start.26 = (bf16[320,1280]{1,0:T(8,128)(2,1)S(1)}, bf16[320,1280]{1,0:T(8,128)(2,1)S(1)}, u32[]{:S(2)}, u32[]{:S(2)}) collective-permute-start(bf16[320,1280]{1,0:T(8,128)(2,1)S(1)} %collective-permute-done.24), channel_id=1, source_target_pairs={{0,28},{4,0},{8,4},{12,8},{16,12},{20,16},{24,20},{28,24},{1,29},{... | collective-permute-start | bytes 2457608 | tf_op jit(solution)/shard_map/ppermute | solution.py:24
  1168.1 99.8 %collective-permute-start.13 = (bf16[160,2560]{1,0:T(8,128)(2,1)S(1)}, bf16[160,2560]{1,0:T(8,128)(2,1)S(1)}, u32[]{:S(2)}, u32[]{:S(2)}) collective-permute-start(bf16[160,2560]{1,0:T(8,128)(2,1)S(1)} %collective-permute-done.11), channel_id=1, source_target_pairs={{0,4},{4,8},{8,12},{12,16},{16,20},{20,24},{24,28},{28,0},{1,5},{5... | collective-permute-start | bytes 2457608 | tf_op jit(solution)/shard_map/ppermute | solution.py:21
  1183.8 86.5 %collective-permute-start.6 = (bf16[160,2560]{1,0:T(8,128)(2,1)S(1)}, bf16[160,2560]{1,0:T(8,128)(2,1)S(1)}, u32[]{:S(2)}, u32[]{:S(2)}) collective-permute-start(bf16[160,2560]{1,0:T(8,128)(2,1)S(1)} %collective-permute-done.4), channel_id=1, source_target_pairs={{0,4},{4,8},{8,12},{12,16},{16,20},{20,24},{24,28},{28,0},{1,5},{5... | collective-permute-start | bytes 2457608 | tf_op jit(solution)/shard_map/ppermute | solution.py:21
  (99 other events, 1778.9 us)
Sparse Core Ops, SparseCore 0:
  11.9 26.9 all-gather.5
  40.4 24.2 all-gather.9
  67.6 8.0 reduce-scatter.13
  78.4 20.1 reduce-scatter.11
  100.7 14.4 reduce-scatter.17
  205.5 64.5 reduce-scatter.27
  272.2 10.3 all-gather.13
  284.7 12.5 all-gather.11
  299.4 12.5 all-gather.7
  314.0 22.5 all-reduce.29
  342.8 122.5 all-reduce.31
  467.5 39.5 reduce-scatter.19
  509.5 38.2 reduce-scatter.15
  551.8 121.6 reduce-scatter.23
  678.0 134.9 reduce-scatter.21
  816.4 135.9 reduce-scatter.25
